TPU v7x, 512 devices: a whole 4x8x8 slice. The times are simulated.
512 devices in a mesh: row: 16 (over x, y_hi), col: 16 (over y_lo, z), img: 2 (over core).
Axes of the slice: x: 4, y: 8 (y_hi: 4, y_lo: 2; y = y_hi * 2 + y_lo), z: 8, core: 2. Of those that a mesh axis runs over, the one named last changes fastest.
Arguments:
- student: bfloat16 [2, 4096, 4096], P('img', 'col', 'row'), may hold values from -6 to 6
- teacher: bfloat16 [2, 4096, 4096], P('img', 'col', 'row'), may hold values from -6 to 6
Outputs:
- feature_grad: bfloat16 [2, 4096, 4096], P('img', 'col', 'row')
All inputs are finite; a program needn't handle non-finite values.
Results may differ from a plain program's by a relative error of at most 0.012.
Values may be sent and summed in bfloat16 or wider, within the bound.
A program may use at most 64 MiB of HBM per device.

v0:
```python
import jax
import jax.numpy as jnp
from jax import lax
from jax.sharding import PartitionSpec as P


def broadcast(value, axis, source):
    kept = jnp.where(lax.axis_index(axis) == source, value, 0).astype(value.dtype)
    return lax.psum(kept, axis)


def body(student, teacher):
    width = student.shape[2] * lax.axis_size("row")
    own_student, own_teacher = (
        lax.all_gather(student, "row", axis=2, tiled=True),
        lax.all_gather(teacher, "row", axis=2, tiled=True),
    )
    got_student, got_teacher = (
        broadcast(own_student, "col", lax.axis_index("row")),
        broadcast(own_teacher, "col", lax.axis_index("row")),
    )
    on_diagonal = lax.axis_index("row") == lax.axis_index("col")
    row_student = jnp.where(on_diagonal, own_student, got_student)
    row_teacher = jnp.where(on_diagonal, own_teacher, got_teacher)
    gram_student = jnp.einsum(
        "ipd,iqd->ipq", row_student, own_student, preferred_element_type=jnp.float32
    )
    gram_teacher = jnp.einsum(
        "ipd,iqd->ipq", row_teacher, own_teacher, preferred_element_type=jnp.float32
    )
    gap = ((gram_student - gram_teacher) / width).astype(jnp.bfloat16)
    partial_term = jnp.einsum("ipq,ipd->iqd", gap, row_student, preferred_element_type=jnp.float32)
    summed = lax.psum_scatter(
        partial_term.astype(jnp.bfloat16), "row", scatter_dimension=2, tiled=True
    )
    return summed


def solution(mesh):
    placed = (P("img", "col", "row"), P("img", "col", "row"))
    return jax.shard_map(
        body, mesh=mesh, in_specs=placed, out_specs=P("img", "col", "row"), check_vma=False
    )
```

profile of v0, /device:TPU:1, one launch (start us, length us, event | category | flops | bytes accessed | tf_op | source)
XLA Modules:
  0.0 422.1 jit_solution(3025703780337332466)
XLA Ops:
  6.5 0.0 all-gather.5.cloned.1.call-start
  6.5 0.7 all-gather.5.cloned.1.call-update
  7.3 0.0 all-gather.3.cloned.1.call-start
  7.3 0.7 all-gather.3.cloned.1.call-update
  8.0 0.0 all-reduce.3.cloned.1.call-start
  8.1 75.4 %all-gather.5.cloned.1.call-done = bf16[1,256,4096]{2,1,0:T(8,128)(2,1)} async-done(((bf16[1,256,256]{2,1,0:T(8,128)(2,1)}), bf16[1,256,4096]{2,1,0:T(8,128)(2,1)}) %all-gather.5.cloned.1.call-update) | async-done | bytes 2097168 | tf_op jit(solution)/shard_map/all_gather | solution.py:16
  83.4 3.1 broadcast_select_fusion
  86.5 67.6 %all-gather.3.cloned.1.call-done = bf16[1,256,4096]{2,1,0:T(8,128)(2,1)} async-done(((bf16[1,256,256]{2,1,0:T(8,128)(2,1)}), bf16[1,256,4096]{2,1,0:T(8,128)(2,1)}) %all-gather.3.cloned.1.call-update) | async-done | bytes 2097168 | tf_op jit(solution)/shard_map/all_gather | solution.py:15
  154.1 3.1 broadcast_select_fusion.1
  157.2 0.0 all-reduce.3.cloned.1.call-update
  157.2 0.0 reduce-scatter.2.cloned.1.call-start
  157.3 150.9 %all-reduce.3.cloned.1.call-done = (bf16[1,256,4096]{2,1,0:T(8,128)(2,1)}, bf16[1,256,4096]{2,1,0:T(8,128)(2,1)}) async-done(((bf16[1,256,4096]{2,1,0:T(8,128)(2,1)}, bf16[1,256,4096]{2,1,0:T(8,128)(2,1)}), (bf16[1,256,4096]{2,1,0:T(8,128)(2,1)}, bf16[1,256,4096]{2,1,0:T(8,128)(2,1)})) %all-reduce.3.cloned.1.call-update) | async-done | bytes 4194320 | tf_op jit(solution)/shard_map/psum | solution.py:9
  308.2 0.0 copy-start
  308.2 3.1 fusion.1
  311.3 0.0 copy-done
  311.3 3.9 fusion
  315.2 0.0 reduce-scatter.2.cloned.1.call-update
  315.2 100.3 %reduce-scatter.2.cloned.1.call-done = bf16[1,256,256]{2,1,0:T(8,128)(2,1)} async-done(((bf16[1,256,4096]{2,1,0:T(8,128)(2,1)}), bf16[1,256,256]{2,1,0:T(8,128)(2,1)}) %reduce-scatter.2.cloned.1.call-update) | async-done | bytes 131088 | tf_op jit(solution)/shard_map/reduce_scatter | solution.py:33
Async XLA Ops:
  6.5 76.9 %all-gather.5.cloned.1.call-start = ((), (), s32[]{:S(2)}) async-start(), calls=%async_computation.2 | async-start | bytes 2228224 | tf_op jit(solution)/shard_map/all_gather | solution.py:16
  7.3 146.8 %all-gather.3.cloned.1.call-start = ((), (), s32[]{:S(2)}) async-start(), calls=%async_computation.1 | async-start | bytes 2228224 | tf_op jit(solution)/shard_map/all_gather | solution.py:15
  8.0 300.2 %all-reduce.3.cloned.1.call-start = ((), (), s32[]{:S(2)}) async-start(), calls=%async_computation.4 | async-start | bytes 8388608 | tf_op jit(solution)/shard_map/psum | solution.py:9
  157.2 258.3 %reduce-scatter.2.cloned.1.call-start = ((), (), s32[]{:S(2)}) async-start(), calls=%async_computation.3 | async-start | bytes 2228224 | tf_op jit(solution)/shard_map/reduce_scatter | solution.py:33
  308.2 3.1 copy-start
Sparse Core Ops, SparseCore 0:
  10.3 73.0 all-gather.4
  86.4 67.6 all-gather.2
  157.3 150.7 all-reduce.2
  315.3 100.1 reduce-scatter.1
where the time goes:
time: 422 us
  waiting for transfers between devices  396 us (94%)
  between operations  13.2 us (3%)
  matrix products  6.98 us (2%)
  other arithmetic  6.16 us (1%)
    psum x1, waiting for transfers between devices, broadcast(): return lax.psum(kept, axis)  151 us
    reduce_scatter x1, waiting for transfers between devices, body(): lax.psum_scatter(partial_term.astype(jnp.bfloat16), 'row', scatter_dimens...  100 us
    all_gather x1, waiting for transfers between devices, body(): lax.all_gather(teacher, 'row', axis=2, tiled=True)  75.4 us
    all_gather x1, waiting for transfers between devices, body(): lax.all_gather(student, 'row', axis=2, tiled=True)  67.6 us
  transfers between devices with their start and end apart: 4, of which 4 were waited for; matrix products, arithmetic and copies ran while one was open for 1% of the time, Pallas kernels for 0%

commit v1 on v0

v1 whole, which is shorter than its diff:
```python
import functools

import jax
import jax.numpy as jnp
from jax import lax
from jax.experimental import pallas as pl
from jax.experimental.pallas import tpu as pltpu
from jax.sharding import PartitionSpec as P

MESH = pl.DeviceIdType.MESH
F32, BF16 = jnp.float32, jnp.bfloat16

COVER = ((0, 0), (0, 1), (0, -2), (1, 2), (1, -2))
CHUNKS = (
    ((0, 0, 256),),
    ((0, 1, 256), (0, 2, 256), (1, 2, 256)),
    ((0, 3, 256), (1, 3, 256), (2, 3, 128)),
    ((1, 4, 256), (2, 4, 128), (3, 4, 128)),
)
WIDTH = sum(w for chunk in CHUNKS for _, _, w in chunk)
COPIES = 8 + 4 + 12 * len(CHUNKS)


def dot(a, b, dims):
    return lax.dot_general(a, b, (dims, ((), ())), preferred_element_type=F32)


def kernel(scale, s_ref, t_ref, out_ref, sb, tb, gs, gf, rx, xs, xf, ry, gg, half, ps, fr, send, recv):
    r, c, img = lax.axis_index("row"), lax.axis_index("col"), lax.axis_index("img")
    x, h, l, z = r // 4, r % 4, c // 8, c % 8
    way = 1 - 2 * img

    def device(dx=0, dh=0, dl=0, dz=0):
        return (
            (x + dx) % 4 * 4 + (h + dh) % 4,
            (l + dl) % 2 * 8 + (z + 8 + way * dz) % 8,
            img,
        )

    count = [0]
    started = []

    def copy(src, dst, to):
        k = count[0]
        count[0] += 1
        made = pltpu.make_async_remote_copy(
            src_ref=src, dst_ref=dst, send_sem=send.at[k], recv_sem=recv.at[k],
            device_id=to, device_id_type=MESH,
        )
        made.start()
        started.append(made)
        return made

    peers = [device(dl=a, dz=b) for a, b in ((0, 1), (0, -2), (1, 1), (1, 0), (0, -1), (0, 2), (1, -2), (1, 2))]
    peers += [device(dx=k) for k in (1, 2, 3)] + [device(dh=k) for k in (1, 2, 3)]
    barrier = pltpu.get_barrier_semaphore()
    for peer in peers:
        pl.semaphore_signal(barrier, inc=1, device_id=peer, device_id_type=MESH)
    pl.semaphore_wait(barrier, len(peers))

    def slot(which, k):
        own, held = ((s_ref, sb), (t_ref, tb))[which]
        return own.at[0] if k == 0 else held.at[k - 1]

    got = {}
    for which in (0, 1):
        got[which, 1] = copy(slot(which, 0), slot(which, 1), device(dz=-1))
        got[which, 2] = copy(slot(which, 0), slot(which, 2), device(dz=2))

    def forward(which):
        got[which, 1].wait_recv()
        got[which, 3] = copy(slot(which, 1), slot(which, 3), device(dl=1, dz=-1))
        got[which, 2].wait_recv()
        got[which, 4] = copy(slot(which, 2), slot(which, 4), device(dl=1))

    def halved(i, j):
        first = (z < 4) if COVER[i][0] == COVER[j][0] else (l == 0)
        f = jnp.where(first, 1, 0)
        rows, columns = i * f + j * (1 - f), j * f + i * (1 - f)
        return rows, columns, pl.multiple_of((1 - f) * 128, 128)

    columns_of = {}
    spans = []
    at = 0
    for chunk in CHUNKS:
        begin = at
        for i, j, w in chunk:
            columns_of[i, j] = pl.ds(at, w)
            at += w
        spans.append(pl.ds(begin, at - begin))

    def gram(n):
        for i, j, w in CHUNKS[n]:
            if w == 256:
                a_s, b_s, a_t, b_t = slot(0, i)[...], slot(0, j)[...], slot(1, i)[...], slot(1, j)[...]
            else:
                rows, columns, begin = halved(i, j)
                a_s, a_t = sb[rows - 1], tb[rows - 1]
                b_s, b_t = sb[columns - 1, pl.ds(begin, 128)], tb[columns - 1, pl.ds(begin, 128)]
            part = (dot(a_s, b_s, ((1,), (1,))) - dot(a_t, b_t, ((1,), (1,)))) * scale
            gf[:, columns_of[i, j]] = part
            gs[:, columns_of[i, j]] = part.astype(BF16)
        for k in (2, 1, 3):
            rows = pl.multiple_of((x + k) % 4 * 64, 64)
            got["sx", n, k] = copy(gs.at[pl.ds(rows, 64), spans[n]], rx.at[k - 1, :, spans[n]], device(dx=k))

    own_x = pl.multiple_of(x * 64, 64)
    own_y = pl.multiple_of(h * 16, 16)
    own = pl.multiple_of(x * 64 + h * 16, 16)

    def sum_x(n):
        for k in (1, 3, 2):
            got["sx", n, k].wait_recv()
        total = gf[pl.ds(own_x, 64), spans[n]]
        for k in range(3):
            total += rx[k, :, spans[n]].astype(F32)
        xf[:, spans[n]] = total
        xs[:, spans[n]] = total.astype(BF16)
        for k in (2, 1, 3):
            rows = pl.multiple_of((h + k) % 4 * 16, 16)
            got["sy", n, k] = copy(xs.at[pl.ds(rows, 16), spans[n]], ry.at[k - 1, :, spans[n]], device(dh=k))

    def sum_y(n):
        for k in (1, 3, 2):
            got["sy", n, k].wait_recv()
        total = xf[pl.ds(own_y, 16), spans[n]]
        for k in range(3):
            total += ry[k, :, spans[n]].astype(F32)
        gg[pl.ds(own, 16), spans[n]] = total.astype(BF16)
        for k in (2, 1, 3):
            piece = gg.at[pl.ds(own, 16), spans[n]]
            got["gy", n, k] = copy(piece, piece, device(dh=k))

    def gather_x(n):
        for k in (1, 3, 2):
            got["gy", n, k].wait_recv()
        for k in (2, 1, 3):
            piece = gg.at[pl.ds(own_x, 64), spans[n]]
            got["gx", n, k] = copy(piece, piece, device(dx=k))

    def arrived(n):
        for k in (1, 3, 2):
            got["gx", n, k].wait_recv()

    gram(0)
    forward(0)
    forward(1)
    gram(1)
    sum_x(0)
    for which in (0, 1):
        got[which, 3].wait_recv()
    gram(2)
    sum_x(1)
    for which in (0, 1):
        got[which, 4].wait_recv()
    gram(3)
    sum_y(0)
    sum_y(1)
    sum_x(2)
    gather_x(0)
    sum_x(3)
    gather_x(1)
    sum_y(2)
    sum_y(3)
    gather_x(2)
    gather_x(3)
    for n in range(len(CHUNKS)):
        arrived(n)

    half[...] = jnp.zeros_like(half)
    for chunk in CHUNKS:
        for i, j, w in chunk:
            if w == 128:
                rows, columns, begin = halved(i, j)
                gap = gg[:, columns_of[i, j]]
                half[rows - 2] += dot(gap, sb[columns - 1, pl.ds(begin, 128)], ((1,), (0,)))
                half[columns - 2, pl.ds(begin, 128)] += dot(gap, sb[rows - 1], ((0,), (0,)))

    def gradient(k):
        total = half[k - 2] if k >= 2 else None
        for chunk in CHUNKS:
            for i, j, w in chunk:
                if w == 256 and k in (i, j):
                    gap = gg[:, columns_of[i, j]]
                    if k == i:
                        term = dot(gap, slot(0, j)[...], ((1,), (0,)))
                    else:
                        term = dot(gap, slot(0, i)[...], ((0,), (0,)))
                    total = term if total is None else total + term
        return total

    for k in (3, 4, 2, 1):
        ps[k - 1] = gradient(k).astype(BF16)
        got["f", k] = copy(ps.at[k - 1], fr.at[k - 1], device(dl=COVER[k][0], dz=COVER[k][1]))
    total = gradient(0)
    for k in (1, 2, 4, 3):
        got["f", k].wait_recv()
        total += fr[k - 1].astype(F32)
    out_ref[0] = total.astype(BF16)
    for made in started:
        made.wait_send()


def body(student, teacher):
    scale = 1.0 / (student.shape[2] * lax.axis_size("row"))
    blocks = pltpu.VMEM((4, 256, 256), BF16)
    return pl.pallas_call(
        functools.partial(kernel, scale),
        out_shape=jax.ShapeDtypeStruct(student.shape, BF16),
        in_specs=[pl.BlockSpec(memory_space=pltpu.VMEM)] * 2,
        out_specs=pl.BlockSpec(memory_space=pltpu.VMEM),
        scratch_shapes=[
            blocks,
            blocks,
            pltpu.VMEM((256, WIDTH), BF16),
            pltpu.VMEM((256, WIDTH), F32),
            pltpu.VMEM((3, 64, WIDTH), BF16),
            pltpu.VMEM((64, WIDTH), BF16),
            pltpu.VMEM((64, WIDTH), F32),
            pltpu.VMEM((3, 16, WIDTH), BF16),
            pltpu.VMEM((256, WIDTH), BF16),
            pltpu.VMEM((3, 256, 256), F32),
            blocks,
            blocks,
            pltpu.SemaphoreType.DMA((COPIES,)),
            pltpu.SemaphoreType.DMA((COPIES,)),
        ],
        compiler_params=pltpu.CompilerParams(
            collective_id=0, has_side_effects=True, vmem_limit_bytes=32 * 1024 * 1024
        ),
    )(student, teacher)


def solution(mesh):
    placed = P("img", "col", "row")
    return jax.shard_map(
        body, mesh=mesh, in_specs=(placed, placed), out_specs=placed, check_vma=False
    )
```

time: 422 us -> 69.2 us (0.16)
  waiting for transfers between devices: 396 us -> 0 us
  Pallas kernels: 0 us -> 66.1 us
  between operations: 13.2 us -> 0.01 us
  matrix products: 6.98 us -> 0 us
  other arithmetic: 6.16 us -> 0 us
    psum x1 -> x0, waiting for transfers between devices: 151 us -> none  [broadcast(): return lax.psum(kept, axis)]
    all_gather x2 -> x0, waiting for transfers between devices: 143 us -> none  [the longest x1 75.4 us: body(): lax.all_gather(teacher, 'row', axis=2, tiled=True)]
    reduce_scatter x1 -> x0, waiting for transfers between devices: 100 us -> none  [body(): lax.psum_scatter(partial_term.astype(jnp.bfloat16), 'row', scatter_dimens...]
    pallas_call x0 -> x1, Pallas kernels: none -> 66.1 us  [body(): pl.pallas_call(functools.partial(kernel, scale), out_shape=jax.ShapeDtype...]
    dot_general x2 -> x0, matrix products: 6.98 us -> none  [the longest x1 3.87 us: body(): jnp.einsum('ipq,ipd->iqd', gap, row_student, preferred_element_type=jnp.f...]
    select_n x2 -> x0, other arithmetic: 6.16 us -> none  [broadcast(): jnp.where(lax.axis_index(axis) == source, value, 0).astype(value.dtype)]
  transfers between devices with their start and end apart: 4 -> 0, of which waited for: 4 -> 0; matrix products, arithmetic and copies ran while one was open for 1% -> 0% of each run, Pallas kernels for 0% -> 0%
where the time goes in v1:
time: 69.2 us; the launch traced here: 68.6 us
  Pallas kernels  66.1 us (96%)
  local copies, waits for them, and re-layouts  2.47 us (4%)
    pallas_call x1, Pallas kernels, body(): pl.pallas_call(functools.partial(kernel, scale), out_shape=jax.ShapeDtype...  66.1 us
    unnamed x5, local copies, waits for them, and re-layouts  2.47 us

profile of v1, /device:TPU:1, one launch (start us, length us, event | category | flops | bytes accessed | tf_op | source)
XLA Modules:
  0.0 68.6 jit_solution(3909542150522677754)
XLA Ops:
  0.0 0.0 copy-start
  0.0 0.9 %copy-done = bf16[1,256,256]{2,1,0:T(8,128)(2,1)S(1)} copy-done((bf16[1,256,256]{2,1,0:T(8,128)(2,1)S(1)}, bf16[1,256,256]{2,1,0:T(8,128)(2,1)}, u32[]{:S(2)}) %copy-start) | copy-done | bytes 131096
  0.9 0.0 copy-start.1
  0.9 0.9 %copy-done.1 = bf16[1,256,256]{2,1,0:T(8,128)(2,1)S(1)} copy-done((bf16[1,256,256]{2,1,0:T(8,128)(2,1)S(1)}, bf16[1,256,256]{2,1,0:T(8,128)(2,1)}, u32[]{:S(2)}) %copy-start.1) | copy-done | bytes 131096
  1.8 66.1 %shard_map.28 = bf16[1,256,256]{2,1,0:T(8,128)(2,1)S(1)} custom-call(bf16[1,256,256]{2,1,0:T(8,128)(2,1)S(1)} %copy-done, bf16[1,256,256]{2,1,0:T(8,128)(2,1)S(1)} %copy-done.1), custom_call_target="tpu_custom_call" | custom-call | tf_op jit(solution)/shard_map/pallas_call | solution.py:207
  67.9 0.7 copy.4
Async XLA Ops:
  0.0 0.9 %copy-start = (bf16[1,256,256]{2,1,0:T(8,128)(2,1)S(1)}, bf16[1,256,256]{2,1,0:T(8,128)(2,1)}, u32[]{:S(2)}) copy-start(bf16[1,256,256]{2,1,0:T(8,128)(2,1)} %s_ref.1) | copy-start | bytes 393220
  0.9 0.9 %copy-start.1 = (bf16[1,256,256]{2,1,0:T(8,128)(2,1)S(1)}, bf16[1,256,256]{2,1,0:T(8,128)(2,1)}, u32[]{:S(2)}) copy-start(bf16[1,256,256]{2,1,0:T(8,128)(2,1)} %t_ref.1) | copy-start | bytes 393220

commit v2 on v1

v2 whole, which is shorter than its diff:
```python
import functools

import jax
import jax.numpy as jnp
from jax import lax
from jax.experimental import pallas as pl
from jax.experimental.pallas import tpu as pltpu
from jax.sharding import PartitionSpec as P

MESH = pl.DeviceIdType.MESH
F32, BF16 = jnp.float32, jnp.bfloat16

COVER = ((0, 0), (0, 1), (0, 3), (0, -1), (1, 0), (1, -1))
CHUNKS = (
    ((0, 0, 256),),
    ((0, 1, 256),),
    ((1, 3, 256), (1, 4, 256), (0, 4, 128)),
    ((1, 5, 256),),
    ((0, 2, 256), (2, 3, 128)),
    ((2, 4, 256), (2, 5, 128)),
)
WHOLE = (3, 4, 5)
WIDTH = sum(w for chunk in CHUNKS for _, _, w in chunk)
HELD = len(COVER)
COPIES = 3 * (HELD - 1) + 12 * len(CHUNKS) - 3 * len(WHOLE)


def dot(a, b, dims):
    return lax.dot_general(a, b, (dims, ((), ())), preferred_element_type=F32)


def kernel(scale, s_ref, t_ref, out_ref, sb, tb, gs, gf, rx, xs, xf, ry, gg, half, ps, fr, send, recv, local):
    r, c, img = lax.axis_index("row"), lax.axis_index("col"), lax.axis_index("img")
    x, h, l, z = r // 4, r % 4, c // 8, c % 8
    way = 1 - 2 * img

    def device(dx=0, dh=0, dl=0, dz=0):
        return (
            (x + dx) % 4 * 4 + (h + dh) % 4,
            (l + dl) % 2 * 8 + (z + 8 + way * dz) % 8,
            img,
        )

    count = [0]
    pending = []

    def copy(src, dst, to):
        k = count[0]
        count[0] += 1
        made = pltpu.make_async_remote_copy(
            src_ref=src, dst_ref=dst, send_sem=send.at[k], recv_sem=recv.at[k],
            device_id=to, device_id_type=MESH,
        )
        made.start()
        pending.append(made)
        return made

    def sent(made):
        pending.remove(made)
        made.wait_send()

    own_copies = [
        pltpu.make_async_copy(ref.at[0], held.at[0], local.at[k])
        for k, (ref, held) in enumerate(((s_ref, sb), (t_ref, tb)))
    ]
    for made in own_copies:
        made.start()

    peers = [device(dl=a, dz=b) for a, b in ((0, 1), (0, -1), (1, 0), (0, 2), (0, -3), (1, 1))]
    peers += [device(dx=k) for k in (1, 2, 3)] + [device(dh=k) for k in (1, 2, 3)]
    barrier = pltpu.get_barrier_semaphore()
    for peer in peers:
        pl.semaphore_signal(barrier, inc=1, device_id=peer, device_id_type=MESH)
    pl.semaphore_wait(barrier, len(peers))

    held = (sb, tb)
    got = {}

    def first(which, k, to):
        own = (s_ref, t_ref)[which].at[0]
        got[which, k] = copy(own, held[which].at[k], to)

    def forward(which, k, to_slot, to):
        got[which, k].wait_recv()
        got[which, to_slot] = copy(held[which].at[k], held[which].at[to_slot], to)

    def halved(i, j):
        first = (z < 4) if COVER[i][0] == COVER[j][0] else (l == 0)
        f = jnp.where(first, 1, 0)
        rows, columns = i * f + j * (1 - f), j * f + i * (1 - f)
        return rows, columns, pl.multiple_of((1 - f) * 128, 128)

    columns_of = {}
    spans = []
    at = 0
    for chunk in CHUNKS:
        begin = at
        for i, j, w in chunk:
            columns_of[i, j] = pl.ds(at, w)
            at += w
        spans.append(pl.ds(begin, at - begin))

    def gram(n):
        for i, j, w in CHUNKS[n]:
            if w == 256:
                a_s, b_s, a_t, b_t = sb[i], sb[j], tb[i], tb[j]
            else:
                rows, columns, begin = halved(i, j)
                a_s, a_t = sb[rows], tb[rows]
                b_s, b_t = sb[columns, pl.ds(begin, 128)], tb[columns, pl.ds(begin, 128)]
            part = (dot(a_s, b_s, ((1,), (1,))) - dot(a_t, b_t, ((1,), (1,)))) * scale
            gf[:, columns_of[i, j]] = part
            gs[:, columns_of[i, j]] = part.astype(BF16)
        for k in (2, 1, 3):
            rows = pl.multiple_of((x + k) % 4 * 64, 64)
            got["sx", n, k] = copy(gs.at[pl.ds(rows, 64), spans[n]], rx.at[k - 1, :, spans[n]], device(dx=k))

    own_x = pl.multiple_of(x * 64, 64)
    own_y = pl.multiple_of(h * 16, 16)
    own = pl.multiple_of(x * 64 + h * 16, 16)

    def sum_x(n):
        for k in (1, 3, 2):
            got["sx", n, k].wait_recv()
        total = gf[pl.ds(own_x, 64), spans[n]]
        for k in range(3):
            total += rx[k, :, spans[n]].astype(F32)
        xf[:, spans[n]] = total
        xs[:, spans[n]] = total.astype(BF16)
        for k in (2, 1, 3):
            if n in WHOLE:
                got["sy", n, k] = copy(xs.at[:, spans[n]], ry.at[k - 1, :, spans[n]], device(dh=k))
            else:
                rows = pl.multiple_of((h + k) % 4 * 16, 16)
                to = ry.at[k - 1, pl.ds(0, 16), spans[n]]
                got["sy", n, k] = copy(xs.at[pl.ds(rows, 16), spans[n]], to, device(dh=k))

    def sum_y(n):
        for k in (1, 3, 2):
            got["sy", n, k].wait_recv()
        if n in WHOLE:
            total = xf[:, spans[n]]
            for k in range(3):
                total += ry[k, :, spans[n]].astype(F32)
            gg[pl.ds(own_x, 64), spans[n]] = total.astype(BF16)
            return
        total = xf[pl.ds(own_y, 16), spans[n]]
        for k in range(3):
            total += ry[k, pl.ds(0, 16), spans[n]].astype(F32)
        gg[pl.ds(own, 16), spans[n]] = total.astype(BF16)
        for k in (2, 1, 3):
            piece = gg.at[pl.ds(own, 16), spans[n]]
            got["gy", n, k] = copy(piece, piece, device(dh=k))

    def gather_x(n):
        if n not in WHOLE:
            for k in (1, 3, 2):
                got["gy", n, k].wait_recv()
        for k in (2, 1, 3):
            piece = gg.at[pl.ds(own_x, 64), spans[n]]
            got["gx", n, k] = copy(piece, piece, device(dx=k))

    def arrived(n):
        for k in (1, 3, 2):
            got["gx", n, k].wait_recv()

    for k, to in ((1, device(dz=-1)), (4, device(dl=1))):
        for which in (0, 1):
            first(which, k, to)
    for made in own_copies:
        made.wait()
    gram(0)
    for which in (0, 1):
        first(which, 3, device(dz=1))
    for which in (0, 1):
        forward(which, 1, 2, device(dz=-2))
    gram(1)
    sum_x(0)
    for which in (0, 1):
        forward(which, 3, 5, device(dl=1))
    for which in (0, 1):
        got[which, 4].wait_recv()
    gram(2)
    sum_x(1)
    sum_y(0)
    for which in (0, 1):
        got[which, 5].wait_recv()
    gram(3)
    for which in (0, 1):
        got[which, 2].wait_recv()
    gram(4)
    gram(5)
    sum_x(2)
    sum_y(1)
    gather_x(0)
    sum_x(3)
    gather_x(1)
    sum_y(2)
    sum_x(4)
    sum_x(5)
    gather_x(2)
    sum_y(3)
    gather_x(3)
    sum_y(4)
    gather_x(4)
    sum_y(5)
    gather_x(5)
    for n in range(4):
        arrived(n)

    def halves(n):
        for i, j, w in CHUNKS[n]:
            if w == 128:
                rows, columns, begin = halved(i, j)
                gap = gg[:, columns_of[i, j]]
                half[rows] += dot(gap, sb[columns, pl.ds(begin, 128)], ((1,), (0,)))
                half[columns, pl.ds(begin, 128)] += dot(gap, sb[rows], ((0,), (0,)))

    def gradient(k):
        total = half[k] if k != 1 else None
        for chunk in CHUNKS:
            for i, j, w in chunk:
                if w == 256 and k in (i, j):
                    gap = gg[:, columns_of[i, j]]
                    if k == i:
                        term = dot(gap, sb[j], ((1,), (0,)))
                    else:
                        term = dot(gap, sb[i], ((0,), (0,)))
                    total = term if total is None else total + term
        return total

    def give(k):
        ps[k - 1] = gradient(k).astype(BF16)
        got["f", k] = copy(ps.at[k - 1], fr.at[k - 1], device(dl=COVER[k][0], dz=COVER[k][1]))

    half[...] = jnp.zeros_like(half)
    halves(2)
    give(1)
    arrived(4)
    halves(4)
    give(3)
    arrived(5)
    halves(5)
    for k in (2, 5, 4):
        give(k)
    total = gradient(0)
    for k in (1, 3, 4, 5, 2):
        got["f", k].wait_recv()
        total += fr[k - 1].astype(F32)
    out_ref[0] = total.astype(BF16)
    for made in pending:
        made.wait_send()


def body(student, teacher):
    scale = 1.0 / (student.shape[2] * lax.axis_size("row"))
    blocks = pltpu.VMEM((HELD, 256, 256), BF16)
    partials = pltpu.VMEM((HELD - 1, 256, 256), BF16)
    return pl.pallas_call(
        functools.partial(kernel, scale),
        out_shape=jax.ShapeDtypeStruct(student.shape, BF16),
        in_specs=[pl.BlockSpec(memory_space=pl.ANY)] * 2,
        out_specs=pl.BlockSpec(memory_space=pltpu.VMEM),
        scratch_shapes=[
            blocks,
            blocks,
            pltpu.VMEM((256, WIDTH), BF16),
            pltpu.VMEM((256, WIDTH), F32),
            pltpu.VMEM((3, 64, WIDTH), BF16),
            pltpu.VMEM((64, WIDTH), BF16),
            pltpu.VMEM((64, WIDTH), F32),
            pltpu.VMEM((3, 64, WIDTH), BF16),
            pltpu.VMEM((256, WIDTH), BF16),
            pltpu.VMEM((HELD, 256, 256), F32),
            partials,
            partials,
            pltpu.SemaphoreType.DMA((COPIES,)),
            pltpu.SemaphoreType.DMA((COPIES,)),
            pltpu.SemaphoreType.DMA((2,)),
        ],
        compiler_params=pltpu.CompilerParams(
            collective_id=0, has_side_effects=True, vmem_limit_bytes=55040 * 1024
        ),
    )(student, teacher)


def solution(mesh):
    placed = P("img", "col", "row")
    return jax.shard_map(
        body, mesh=mesh, in_specs=(placed, placed), out_specs=placed, check_vma=False
    )
```

time: 69.2 us -> 64 us (0.925)
  the two profiles are of different devices: /device:TPU:1 before, /device:TPU:64 now
where the time goes in v2:
time: 64 us; the launch traced here: 63.9 us
  Pallas kernels  63.2 us (99%)
  local copies, waits for them, and re-layouts  0.66 us (1%)
    pallas_call x1, Pallas kernels, body(): pl.pallas_call(functools.partial(kernel, scale), out_shape=jax.ShapeDtype...  63.2 us

profile of v2, /device:TPU:64, one launch (start us, length us, event | category | flops | bytes accessed | tf_op | source)
XLA Modules:
  0.0 63.9 jit_solution(11844494676930733747)
XLA Ops:
  0.0 63.2 %shard_map.28 = bf16[1,256,256]{2,1,0:T(8,128)(2,1)S(1)} custom-call(bf16[1,256,256]{2,1,0:T(8,128)(2,1)} %s_ref.1, bf16[1,256,256]{2,1,0:T(8,128)(2,1)} %t_ref.1), custom_call_target="tpu_custom_call" | custom-call | tf_op jit(solution)/shard_map/pallas_call | solution.py:259
  63.2 0.7 %copy.4 = bf16[1,256,256]{2,1,0:T(8,128)(2,1)} copy(bf16[1,256,256]{2,1,0:T(8,128)(2,1)S(1)} %shard_map.28) | data formatting | bytes 262144

commit v3 on v2

--- a/solution.py
+++ b/solution.py
@@ -20,7 +20,7 @@
     ((2, 4, 256), (2, 5, 128)),
 )
 WHOLE = (3, 4, 5)
-WIDTH = sum(w for chunk in CHUNKS for _, _, w in chunk)
+WIDTHS = [sum(w for _, _, w in chunk) for chunk in CHUNKS]
 HELD = len(COVER)
 COPIES = 3 * (HELD - 1) + 12 * len(CHUNKS) - 3 * len(WHOLE)
 
@@ -66,7 +66,7 @@
     for made in own_copies:
         made.start()
 
-    peers = [device(dl=a, dz=b) for a, b in ((0, 1), (0, -1), (1, 0), (0, 2), (0, -3), (1, 1))]
+    peers = [device(dl=a, dz=b) for a, b in ((0, 1), (0, -1), (1, 0), (0, 2))]
     peers += [device(dx=k) for k in (1, 2, 3)] + [device(dh=k) for k in (1, 2, 3)]
     barrier = pltpu.get_barrier_semaphore()
     for peer in peers:
@@ -90,15 +90,12 @@
         rows, columns = i * f + j * (1 - f), j * f + i * (1 - f)
         return rows, columns, pl.multiple_of((1 - f) * 128, 128)
 
-    columns_of = {}
-    spans = []
-    at = 0
-    for chunk in CHUNKS:
-        begin = at
+    place = {}
+    for n, chunk in enumerate(CHUNKS):
+        at = 0
         for i, j, w in chunk:
-            columns_of[i, j] = pl.ds(at, w)
+            place[i, j] = n, pl.ds(at, w)
             at += w
-        spans.append(pl.ds(begin, at - begin))
 
     def gram(n):
         for i, j, w in CHUNKS[n]:
@@ -109,11 +106,11 @@
                 a_s, a_t = sb[rows], tb[rows]
                 b_s, b_t = sb[columns, pl.ds(begin, 128)], tb[columns, pl.ds(begin, 128)]
             part = (dot(a_s, b_s, ((1,), (1,))) - dot(a_t, b_t, ((1,), (1,)))) * scale
-            gf[:, columns_of[i, j]] = part
-            gs[:, columns_of[i, j]] = part.astype(BF16)
+            gf[n][:, place[i, j][1]] = part
+            gs[n][:, place[i, j][1]] = part.astype(BF16)
         for k in (2, 1, 3):
             rows = pl.multiple_of((x + k) % 4 * 64, 64)
-            got["sx", n, k] = copy(gs.at[pl.ds(rows, 64), spans[n]], rx.at[k - 1, :, spans[n]], device(dx=k))
+            got["sx", n, k] = copy(gs[n].at[pl.ds(rows, 64)], rx[n].at[k - 1], device(dx=k))
 
     own_x = pl.multiple_of(x * 64, 64)
     own_y = pl.multiple_of(h * 16, 16)
@@ -122,34 +119,34 @@
     def sum_x(n):
         for k in (1, 3, 2):
             got["sx", n, k].wait_recv()
-        total = gf[pl.ds(own_x, 64), spans[n]]
+        total = gf[n][pl.ds(own_x, 64)]
         for k in range(3):
-            total += rx[k, :, spans[n]].astype(F32)
-        xf[:, spans[n]] = total
-        xs[:, spans[n]] = total.astype(BF16)
+            total += rx[n][k].astype(F32)
+        xf[n][...] = total
+        xs[n][...] = total.astype(BF16)
         for k in (2, 1, 3):
             if n in WHOLE:
-                got["sy", n, k] = copy(xs.at[:, spans[n]], ry.at[k - 1, :, spans[n]], device(dh=k))
+                got["sy", n, k] = copy(xs[n], ry[n].at[k - 1], device(dh=k))
             else:
                 rows = pl.multiple_of((h + k) % 4 * 16, 16)
-                to = ry.at[k - 1, pl.ds(0, 16), spans[n]]
-                got["sy", n, k] = copy(xs.at[pl.ds(rows, 16), spans[n]], to, device(dh=k))
+                to = ry[n].at[k - 1, pl.ds(0, 16)]
+                got["sy", n, k] = copy(xs[n].at[pl.ds(rows, 16)], to, device(dh=k))
 
     def sum_y(n):
         for k in (1, 3, 2):
             got["sy", n, k].wait_recv()
         if n in WHOLE:
-            total = xf[:, spans[n]]
+            total = xf[n][...]
             for k in range(3):
-                total += ry[k, :, spans[n]].astype(F32)
-            gg[pl.ds(own_x, 64), spans[n]] = total.astype(BF16)
+                total += ry[n][k].astype(F32)
+            gg[n][pl.ds(own_x, 64)] = total.astype(BF16)
             return
-        total = xf[pl.ds(own_y, 16), spans[n]]
+        total = xf[n][pl.ds(own_y, 16)]
         for k in range(3):
-            total += ry[k, pl.ds(0, 16), spans[n]].astype(F32)
-        gg[pl.ds(own, 16), spans[n]] = total.astype(BF16)
-        for k in (2, 1, 3):
-            piece = gg.at[pl.ds(own, 16), spans[n]]
+            total += ry[n][k, pl.ds(0, 16)].astype(F32)
+        gg[n][pl.ds(own, 16)] = total.astype(BF16)
+        for k in (2, 1, 3):
+            piece = gg[n].at[pl.ds(own, 16)]
             got["gy", n, k] = copy(piece, piece, device(dh=k))
 
     def gather_x(n):
@@ -157,7 +154,7 @@
             for k in (1, 3, 2):
                 got["gy", n, k].wait_recv()
         for k in (2, 1, 3):
-            piece = gg.at[pl.ds(own_x, 64), spans[n]]
+            piece = gg[n].at[pl.ds(own_x, 64)]
             got["gx", n, k] = copy(piece, piece, device(dx=k))
 
     def arrived(n):
@@ -190,6 +187,7 @@
         got[which, 2].wait_recv()
     gram(4)
     gram(5)
+    half[...] = jnp.zeros_like(half)
     sum_x(2)
     sum_y(1)
     gather_x(0)
@@ -198,9 +196,9 @@
     sum_y(2)
     sum_x(4)
     sum_x(5)
-    gather_x(2)
     sum_y(3)
     gather_x(3)
+    gather_x(2)
     sum_y(4)
     gather_x(4)
     sum_y(5)
@@ -212,44 +210,48 @@
         for i, j, w in CHUNKS[n]:
             if w == 128:
                 rows, columns, begin = halved(i, j)
-                gap = gg[:, columns_of[i, j]]
+                gap = gg[place[i, j][0]][:, place[i, j][1]]
                 half[rows] += dot(gap, sb[columns, pl.ds(begin, 128)], ((1,), (0,)))
                 half[columns, pl.ds(begin, 128)] += dot(gap, sb[rows], ((0,), (0,)))
 
-    def gradient(k):
-        total = half[k] if k != 1 else None
-        for chunk in CHUNKS:
-            for i, j, w in chunk:
+    def gradient(k, chunks):
+        total = half[k]
+        for n in chunks:
+            for i, j, w in CHUNKS[n]:
                 if w == 256 and k in (i, j):
-                    gap = gg[:, columns_of[i, j]]
+                    gap = gg[n][:, place[i, j][1]]
                     if k == i:
-                        term = dot(gap, sb[j], ((1,), (0,)))
+                        total = total + dot(gap, sb[j], ((1,), (0,)))
                     else:
-                        term = dot(gap, sb[i], ((0,), (0,)))
-                    total = term if total is None else total + term
+                        total = total + dot(gap, sb[i], ((0,), (0,)))
         return total
 
-    def give(k):
-        ps[k - 1] = gradient(k).astype(BF16)
+    def give(k, chunks):
+        ps[k - 1] = gradient(k, chunks).astype(BF16)
         got["f", k] = copy(ps.at[k - 1], fr.at[k - 1], device(dl=COVER[k][0], dz=COVER[k][1]))
 
-    half[...] = jnp.zeros_like(half)
     halves(2)
-    give(1)
+    give(1, range(4))
     arrived(4)
     halves(4)
-    give(3)
+    give(3, range(5))
+    for k in (2, 5, 4, 0):
+        half[k] = gradient(k, range(5))
     arrived(5)
     halves(5)
     for k in (2, 5, 4):
-        give(k)
-    total = gradient(0)
+        give(k, (5,))
+    total = half[0]
     for k in (1, 3, 4, 5, 2):
         got["f", k].wait_recv()
         total += fr[k - 1].astype(F32)
     out_ref[0] = total.astype(BF16)
     for made in pending:
         made.wait_send()
+
+
+def by_chunk(shape, dtype):
+    return tuple(pltpu.VMEM((*shape, w), dtype) for w in WIDTHS)
 
 
 def body(student, teacher):
@@ -264,13 +266,13 @@
         scratch_shapes=[
             blocks,
             blocks,
-            pltpu.VMEM((256, WIDTH), BF16),
-            pltpu.VMEM((256, WIDTH), F32),
-            pltpu.VMEM((3, 64, WIDTH), BF16),
-            pltpu.VMEM((64, WIDTH), BF16),
-            pltpu.VMEM((64, WIDTH), F32),
-            pltpu.VMEM((3, 64, WIDTH), BF16),
-            pltpu.VMEM((256, WIDTH), BF16),
+            by_chunk((256,), BF16),
+            by_chunk((256,), F32),
+            by_chunk((3, 64), BF16),
+            by_chunk((64,), BF16),
+            by_chunk((64,), F32),
+            by_chunk((3, 64), BF16),
+            by_chunk((256,), BF16),
             pltpu.VMEM((HELD, 256, 256), F32),
             partials,
             partials,

time: 64 us -> 63.2 us (0.988)
  the two profiles are of different devices: /device:TPU:64 before, /device:TPU:1 now
where the time goes in v3:
time: 63.2 us; the launch traced here: 62 us
  Pallas kernels  61.3 us (97%)
  local copies, waits for them, and re-layouts  0.66 us (1%)
    pallas_call x1, Pallas kernels, body(): pl.pallas_call(functools.partial(kernel, scale), out_shape=jax.ShapeDtype...  61.3 us

profile of v3, /device:TPU:1, one launch (start us, length us, event | category | flops | bytes accessed | tf_op | source)
XLA Modules:
  0.0 62.0 jit_solution(2915564882043721731)
XLA Ops:
  0.0 61.3 %shard_map.28 = bf16[1,256,256]{2,1,0:T(8,128)(2,1)S(1)} custom-call(bf16[1,256,256]{2,1,0:T(8,128)(2,1)} %s_ref.1, bf16[1,256,256]{2,1,0:T(8,128)(2,1)} %t_ref.1), custom_call_target="tpu_custom_call" | custom-call | tf_op jit(solution)/shard_map/pallas_call | solution.py:261
  61.3 0.7 %copy.4 = bf16[1,256,256]{2,1,0:T(8,128)(2,1)} copy(bf16[1,256,256]{2,1,0:T(8,128)(2,1)S(1)} %shard_map.28) | data formatting | bytes 262144

commit v4 on v3

--- a/solution.py
+++ b/solution.py
@@ -182,28 +182,28 @@
     sum_y(0)
     for which in (0, 1):
         got[which, 5].wait_recv()
-    gram(3)
     for which in (0, 1):
         got[which, 2].wait_recv()
     gram(4)
     gram(5)
+    gram(3)
     half[...] = jnp.zeros_like(half)
     sum_x(2)
     sum_y(1)
     gather_x(0)
-    sum_x(3)
+    sum_x(4)
     gather_x(1)
     sum_y(2)
-    sum_x(4)
     sum_x(5)
+    sum_x(3)
+    sum_y(4)
+    gather_x(4)
+    gather_x(2)
+    sum_y(5)
+    gather_x(5)
     sum_y(3)
     gather_x(3)
-    gather_x(2)
-    sum_y(4)
-    gather_x(4)
-    sum_y(5)
-    gather_x(5)
-    for n in range(4):
+    for n in (0, 1, 2, 4):
         arrived(n)
 
     def halves(n):
@@ -231,18 +231,21 @@
         got["f", k] = copy(ps.at[k - 1], fr.at[k - 1], device(dl=COVER[k][0], dz=COVER[k][1]))
 
     halves(2)
-    give(1, range(4))
-    arrived(4)
     halves(4)
-    give(3, range(5))
-    for k in (2, 5, 4, 0):
-        half[k] = gradient(k, range(5))
+    give(3, (2,))
+    for k in (2, 4):
+        half[k] = gradient(k, (2, 4))
     arrived(5)
     halves(5)
-    for k in (2, 5, 4):
-        give(k, (5,))
+    give(2, (5,))
+    give(4, (5,))
+    half[0] = gradient(0, (0, 1, 2, 4))
+    half[1] = gradient(1, (1, 2))
+    arrived(3)
+    give(5, (3,))
+    give(1, (3,))
     total = half[0]
-    for k in (1, 3, 4, 5, 2):
+    for k in (3, 4, 2, 1, 5):
         got["f", k].wait_recv()
         total += fr[k - 1].astype(F32)
     out_ref[0] = total.astype(BF16)

time: 63.2 us -> 62.8 us (level); the launches traced: 62 us -> 62.3 us
  no operation moved by 1% of the time
where the time goes in v4:
time: 62.8 us; the launch traced here: 62.3 us
  Pallas kernels  61.7 us (98%)
  local copies, waits for them, and re-layouts  0.66 us (1%)
    pallas_call x1, Pallas kernels, body(): pl.pallas_call(functools.partial(kernel, scale), out_shape=jax.ShapeDtype...  61.7 us

profile of v4, /device:TPU:1, one launch (start us, length us, event | category | flops | bytes accessed | tf_op | source)
XLA Modules:
  0.0 62.3 jit_solution(3781975235177221273)
XLA Ops:
  0.0 61.7 %shard_map.28 = bf16[1,256,256]{2,1,0:T(8,128)(2,1)S(1)} custom-call(bf16[1,256,256]{2,1,0:T(8,128)(2,1)} %s_ref.1, bf16[1,256,256]{2,1,0:T(8,128)(2,1)} %t_ref.1), custom_call_target="tpu_custom_call" | custom-call | tf_op jit(solution)/shard_map/pallas_call | solution.py:264
  61.7 0.7 %copy.4 = bf16[1,256,256]{2,1,0:T(8,128)(2,1)} copy(bf16[1,256,256]{2,1,0:T(8,128)(2,1)S(1)} %shard_map.28) | data formatting | bytes 262144

commit v5 on v4

--- a/solution.py
+++ b/solution.py
@@ -97,15 +97,19 @@
             place[i, j] = n, pl.ds(at, w)
             at += w
 
+    def products(held_blocks, i, j, w):
+        if w == 256:
+            return dot(held_blocks[i], held_blocks[j], ((1,), (1,)))
+        rows, columns, begin = halved(i, j)
+        return dot(held_blocks[rows], held_blocks[columns, pl.ds(begin, 128)], ((1,), (1,)))
+
+    def gram_student(n):
+        for i, j, w in CHUNKS[n]:
+            gf[n][:, place[i, j][1]] = products(sb, i, j, w)
+
     def gram(n):
         for i, j, w in CHUNKS[n]:
-            if w == 256:
-                a_s, b_s, a_t, b_t = sb[i], sb[j], tb[i], tb[j]
-            else:
-                rows, columns, begin = halved(i, j)
-                a_s, a_t = sb[rows], tb[rows]
-                b_s, b_t = sb[columns, pl.ds(begin, 128)], tb[columns, pl.ds(begin, 128)]
-            part = (dot(a_s, b_s, ((1,), (1,))) - dot(a_t, b_t, ((1,), (1,)))) * scale
+            part = (gf[n][:, place[i, j][1]] - products(tb, i, j, w)) * scale
             gf[n][:, place[i, j][1]] = part
             gs[n][:, place[i, j][1]] = part.astype(BF16)
         for k in (2, 1, 3):
@@ -166,25 +170,30 @@
             first(which, k, to)
     for made in own_copies:
         made.wait()
+    gram_student(0)
     gram(0)
     for which in (0, 1):
         first(which, 3, device(dz=1))
     for which in (0, 1):
         forward(which, 1, 2, device(dz=-2))
+    gram_student(1)
     gram(1)
     sum_x(0)
     for which in (0, 1):
         forward(which, 3, 5, device(dl=1))
     for which in (0, 1):
         got[which, 4].wait_recv()
+    gram_student(2)
     gram(2)
     sum_x(1)
     sum_y(0)
-    for which in (0, 1):
-        got[which, 5].wait_recv()
-    for which in (0, 1):
-        got[which, 2].wait_recv()
+    got[0, 5].wait_recv()
+    got[0, 2].wait_recv()
+    for n in (4, 5, 3):
+        gram_student(n)
+    got[1, 2].wait_recv()
     gram(4)
+    got[1, 5].wait_recv()
     gram(5)
     gram(3)
     half[...] = jnp.zeros_like(half)

time: 62.8 us -> 62.7 us (level)
  the two profiles are of different devices: /device:TPU:1 before, /device:TPU:56 now
where the time goes in v5:
time: 62.7 us; the launch traced here: 62.6 us
  Pallas kernels  61.9 us (99%)
  local copies, waits for them, and re-layouts  0.66 us (1%)
    pallas_call x1, Pallas kernels, body(): pl.pallas_call(functools.partial(kernel, scale), out_shape=jax.ShapeDtype...  61.9 us

profile of v5, /device:TPU:56, one launch (start us, length us, event | category | flops | bytes accessed | tf_op | source)
XLA Modules:
  0.0 62.6 jit_solution(8606689396893568644)
XLA Ops:
  0.0 61.9 %shard_map.28 = bf16[1,256,256]{2,1,0:T(8,128)(2,1)S(1)} custom-call(bf16[1,256,256]{2,1,0:T(8,128)(2,1)} %s_ref.1, bf16[1,256,256]{2,1,0:T(8,128)(2,1)} %t_ref.1), custom_call_target="tpu_custom_call" | custom-call | tf_op jit(solution)/shard_map/pallas_call | solution.py:273
  62.0 0.7 %copy.4 = bf16[1,256,256]{2,1,0:T(8,128)(2,1)} copy(bf16[1,256,256]{2,1,0:T(8,128)(2,1)S(1)} %shard_map.28) | data formatting | bytes 262144
